TPU v7x, 256 devices: a whole 4x4x8 slice. The times are simulated.
256 devices in a mesh: pair: 32 (over x, y, core), int: 8 (over z).
Axes of the slice: x: 4, y: 4, z: 8, core: 2. Of those that a mesh axis runs over, the one named last changes fastest.
Arguments:
- amplitudes: float32 [2, 3072, 3072], P(None, 'pair', 'int'), as said below
- integrals: float32 [2, 3072, 3072], P(None, 'pair', 'int'), as said below
Outputs:
- residual: float32 [2, 3072, 3072], P(None, 'pair', 'int')
Inputs may be any that keep to these rules, and one draw needn't show every extreme that they name: Every class block is exactly symmetric: amplitudes[h, p, q] equals amplitudes[h, q, p]. Every class block is exactly symmetric: integrals[h, p, q] equals integrals[h, q, p].
All inputs are finite; a program needn't handle non-finite values.
Results may differ from a plain program's by a relative error of at most 0.000053.
Values sent between devices are 32-bit elements; how exact they have to be, the bound alone decides.
A program may use at most 128 MiB of HBM per device.

v0:
```python
import jax
import jax.numpy as jnp
from jax import lax
from jax.sharding import PartitionSpec as P


def shards(amplitudes, integrals):
    highest = lax.Precision.HIGHEST
    column_terms = jnp.einsum(
        "hkl,hbl->hkb",
        lax.all_gather(amplitudes, "pair", axis=1, tiled=True),
        integrals,
        precision=highest,
    )
    column_share = lax.psum_scatter(column_terms, "int", scatter_dimension=1, tiled=True)
    cycle_inter = jnp.transpose(integrals, (0, 2, 1)) + column_share
    row_block = lax.all_gather(amplitudes, "int", axis=2, tiled=True)
    row_share = lax.psum_scatter(
        jnp.einsum("hak,hkb->bha", cycle_inter, row_block, precision=highest),
        "pair",
        scatter_dimension=0,
        tiled=True,
    )
    return jnp.transpose(cycle_inter, (0, 2, 1)) + jnp.transpose(row_share, (1, 0, 2))


def solution(mesh):
    placed = (P(None, "pair", "int"), P(None, "pair", "int"))
    return jax.shard_map(
        shards, mesh=mesh, in_specs=placed, out_specs=P(None, "pair", "int"), check_vma=False
    )
```

profile of v0, /device:TPU:1, one launch (start us, length us, event | category | flops | bytes accessed | tf_op | source)
XLA Modules:
  0.0 282.2 jit_solution(12278914163022216258)
XLA Ops:
  6.5 0.0 copy-start
  6.5 0.0 all-gather.3.cloned.1.call-start
  6.5 0.7 all-gather.3.cloned.1.call-update
  7.3 0.0 all-gather.5.cloned.1.call-start
  7.3 0.7 all-gather.5.cloned.1.call-update
  8.0 0.0 reduce-scatter.3.cloned.1.call-start
  8.1 66.6 %all-gather.3.cloned.1.call-done = f32[2,3072,384]{2,1,0:T(8,128)} async-done(((f32[2,96,384]{2,1,0:T(8,128)}), f32[2,3072,384]{2,1,0:T(8,128)}) %all-gather.3.cloned.1.call-update) | async-done | bytes 9437200 | tf_op jit(solution)/shard_map/all_gather | solution.py:11
  74.6 12.8 %fusion = f32[2,3072,96]{1,2,0:T(8,128)} fusion(f32[2,3072,384]{2,1,0:T(8,128)} %all-gather.3.cloned.1.call-done, f32[2,96,384]{2,1,0:T(8,128)} %param.3), kind=kOutput, calls=%fused_computation.3 | convolution fusion | flops 2717908992 | bytes 12091392 | tf_op jit(solution)/shard_map/hkl,hbl->hkb/dot_general | solution.py:9
  87.5 0.0 reduce-scatter.3.cloned.1.call-update
  87.5 0.0 reduce-scatter.5.cloned.1.call-start
  87.5 26.8 %all-gather.5.cloned.1.call-done = f32[2,96,3072]{2,1,0:T(8,128)} async-done(((f32[2,96,384]{2,1,0:T(8,128)}), f32[2,96,3072]{2,1,0:T(8,128)}) %all-gather.5.cloned.1.call-update) | async-done | bytes 2359312 | tf_op jit(solution)/shard_map/all_gather | solution.py:17
  114.3 43.1 %reduce-scatter.3.cloned.1.call-done = f32[2,384,96]{1,2,0:T(8,128)} async-done(((f32[2,3072,96]{1,2,0:T(8,128)}), f32[2,384,96]{1,2,0:T(8,128)}) %reduce-scatter.3.cloned.1.call-update) | async-done | bytes 294928 | tf_op jit(solution)/shard_map/reduce_scatter | solution.py:15
  157.5 0.0 copy-done
  157.5 0.0 copy-start.1
  157.5 11.4 %convolution_bitcast_fusion = f32[3072,2,384]{2,0,1:T(8,128)} fusion(f32[2,96,3072]{2,1,0:T(8,128)} %all-gather.5.cloned.1.call-done, f32[2,384,96]{1,2,0:T(8,128)} %reduce-scatter.3.cloned.1.call-done, f32[2,96,384]{2,1,0:T(8,128)S(1)} %copy-done), kind=kOutput, calls=%fused_computation | convolution fusion | flops 2717982720 | bytes 12386304 | tf_op jit(solution)/shard_map/hak,hkb->bha/dot_general | solution.py:19
  168.9 0.0 reduce-scatter.5.cloned.1.call-update
  169.0 105.0 %reduce-scatter.5.cloned.1.call-done = f32[96,2,384]{2,0,1:T(8,128)} async-done(((f32[3072,2,384]{2,0,1:T(8,128)}), f32[96,2,384]{2,0,1:T(8,128)}) %reduce-scatter.5.cloned.1.call-update) | async-done | bytes 294928 | tf_op jit(solution)/shard_map/reduce_scatter | solution.py:18
  273.9 0.0 copy-done.1
  273.9 1.7 bitcast_add_fusion
Async XLA Ops:
  6.5 151.0 %copy-start = (f32[2,96,384]{2,1,0:T(8,128)S(1)}, f32[2,96,384]{2,1,0:T(8,128)}, u32[]{:S(2)}) copy-start(f32[2,96,384]{2,1,0:T(8,128)} %param.3) | copy-start | bytes 884740
  6.5 68.1 %all-gather.3.cloned.1.call-start = ((), (), s32[]{:S(2)}) async-start(), calls=%async_computation.2 | async-start | bytes 9732096 | tf_op jit(solution)/shard_map/all_gather | solution.py:11
  7.3 107.1 %all-gather.5.cloned.1.call-start = ((), (), s32[]{:S(2)}) async-start(), calls=%async_computation.4 | async-start | bytes 2654208 | tf_op jit(solution)/shard_map/all_gather | solution.py:17
  8.0 149.5 %reduce-scatter.3.cloned.1.call-start = ((), (), s32[]{:S(2)}) async-start(), calls=%async_computation.3 | async-start | bytes 2654208 | tf_op jit(solution)/shard_map/reduce_scatter | solution.py:15
  87.5 186.4 %reduce-scatter.5.cloned.1.call-start = ((), (), s32[]{:S(2)}) async-start(), calls=%async_computation.5 | async-start | bytes 9732096 | tf_op jit(solution)/shard_map/reduce_scatter | solution.py:18
  157.5 116.4 %copy-start.1 = (f32[2,384,96]{1,2,0:T(8,128)S(1)}, f32[2,384,96]{1,2,0:T(8,128)}, u32[]{:S(2)}) copy-start(f32[2,384,96]{1,2,0:T(8,128)} %reduce-scatter.3.cloned.1.call-done) | copy-start | bytes 884740
Sparse Core Ops, SparseCore 0:
  9.9 64.6 all-gather.2
  76.4 37.8 all-gather.4
  116.9 40.5 reduce-scatter.2
  169.1 104.7 reduce-scatter.4
where the time goes:
time: 283 us; the launch traced here: 282 us
  waiting for transfers between devices  243 us (86%)
  matrix products  24.3 us (9%)
  between operations  13.1 us (5%)
    reduce_scatter x1, waiting for transfers between devices, shards(): lax.psum_scatter(jnp.einsum('hak,hkb->bha', cycle_inter, row_block, preci...  105 us
    all_gather x1, waiting for transfers between devices, shards(): lax.all_gather(amplitudes, 'pair', axis=1, tiled=True)  66.6 us
    reduce_scatter x1, waiting for transfers between devices, shards(): lax.psum_scatter(column_terms, 'int', scatter_dimension=1, tiled=True)  43.1 us
    all_gather x1, waiting for transfers between devices, shards(): row_block = lax.all_gather(amplitudes, 'int', axis=2, tiled=True)  26.8 us
    dot_general x1, matrix products, shards(): jnp.einsum('hkl,hbl->hkb', lax.all_gather(amplitudes, 'pair', axis=1, til...  12.8 us
    dot_general x1, matrix products, shards(): jnp.einsum('hak,hkb->bha', cycle_inter, row_block, precision=highest)  11.4 us
  transfers between devices with their start and end apart: 4, of which 4 were waited for; matrix products, arithmetic and copies ran while one was open for 5% of the time, Pallas kernels for 0%

commit v1 on v0

v1 whole, which is shorter than its diff:
```python
import functools

import jax
import jax.numpy as jnp
from jax import lax
from jax.experimental import pallas as pl
from jax.experimental.pallas import tpu as pltpu
from jax.sharding import PartitionSpec as P

MESH = pl.DeviceIdType.MESH


def split(v):
    high = v.astype(jnp.bfloat16)
    return high, (v - high.astype(jnp.float32)).astype(jnp.bfloat16)


def product(a, b):
    a_high, a_low = split(a)
    b_high, b_low = split(b)
    dot = functools.partial(jnp.dot, preferred_element_type=jnp.float32)
    return dot(a_high, b_high) + (dot(a_high, b_low) + dot(a_low, b_high))


def kernel(
    nx, ny, nz, a_ref, i_ref, o_ref,
    x_rows, i_cols, a_cols, t_rows, total, theirs,
    send_sem, local_sem, x_sem, i_sem, a_sem, t_sem, r_sem,
):
    rows = a_ref.shape[1]
    width = a_ref.shape[2]
    pair, z = lax.axis_index("pair"), lax.axis_index("int")
    c = lax.rem(pair, 2)
    chip = pair // 2
    y, x = lax.rem(chip, ny), chip // ny
    s = 1 - 2 * c

    def device(dx, dy, dz, core):
        xx, yy = lax.rem(x + dx + nx, nx), lax.rem(y + dy + ny, ny)
        zz = lax.rem(z + dz + nz, nz)
        return {"pair": (xx * ny + yy) * 2 + core, "int": zz}

    peers = [device(0, 0, 0, 1 - c)]
    for core in (0, 1):
        for d in (1, -1):
            peers += [device(d, 0, 0, core), device(0, d, 0, core), device(0, 0, d, core)]
    barrier = pltpu.get_barrier_semaphore()
    for peer in peers:
        pl.semaphore_signal(barrier, inc=1, device_id=peer, device_id_type=MESH)
    pl.semaphore_wait(barrier, len(peers))

    started = []

    def send(src, dst, sem, to):
        copy = pltpu.make_async_remote_copy(
            src_ref=src, dst_ref=dst, send_sem=send_sem.at[len(started)], recv_sem=sem,
            device_id=to, device_id_type=MESH,
        )
        copy.start()
        started.append(copy)

    def arrived(ref, sem):
        pltpu.make_async_remote_copy(
            src_ref=ref, dst_ref=ref, send_sem=send_sem.at[0], recv_sem=sem,
            device_id=peers[0], device_id_type=MESH,
        ).wait_recv()

    def keep(src, dst, k):
        copy = pltpu.make_async_copy(src, dst, local_sem.at[k])
        copy.start()
        return copy

    def z_slot(part, dz):
        at = lax.rem(z - dz + nz, nz)
        return x_rows.at[at, part], x_sem.at[part, at]

    def z_first():
        slot, sem = x_rows.at[z, c], x_sem.at[c, z]
        for h in (0, 1):
            for d in (1, -1):
                send(a_ref.at[h], slot, sem, device(0, 0, d, h))
        send(a_ref.at[1 - c], slot, sem, device(0, 0, 0, 1 - c))

    def z_step(k):
        for part in (0, 1):
            slot, sem = z_slot(part, s * k)
            arrived(slot, sem)
            if k < nz // 2:
                send(slot, slot, sem, device(0, 0, s, c))
        if k < nz // 2:
            for part in (0, 1):
                slot, sem = z_slot(part, -s * k)
                arrived(slot, sem)
                if k + 1 < nz // 2:
                    send(slot, slot, sem, device(0, 0, -s, c))

    def xy_slot(buf, sems, part, first, second):
        dx, dy = (first, second) if part == 0 else (second, first)
        at = lax.rem(x - dx + nx, nx) * ny + lax.rem(y - dy + ny, ny)
        return buf.at[at, part], sems.at[part, at]

    def xy_to(part, first, second):
        return device(first, second, 0, c) if part == 0 else device(second, first, 0, c)

    def xy_first(ref, buf, sems):
        at = x * ny + y
        slot, sem = buf.at[at, c], sems.at[c, at]
        for d in (1, -1):
            for h in (0, 1):
                send(ref.at[h], slot, sem, device(d * (1 - c), d * c, 0, h))
        send(ref.at[1 - c], slot, sem, device(0, 0, 0, 1 - c))
        for d in (1, -1):
            for h in (0, 1):
                send(ref.at[h], slot, sem, device(d * c, d * (1 - c), 0, h))

    def xy_forward(buf, sems, part, first, second, along):
        slot, sem = xy_slot(buf, sems, part, first, second)
        arrived(slot, sem)
        for f, g in along:
            send(slot, slot, sem, xy_to(part, f, g))

    def xy_level(buf, sems, level):
        go = functools.partial(xy_forward, buf, sems)
        if level == 1:
            for part in (0, 1):
                go(part, s, 0, [(s, 0), (0, 1), (0, -1)])
            for part in (0, 1):
                go(part, -s, 0, [(0, 1), (0, -1)])
        elif level == 2:
            for part in (0, 1):
                go(part, 2 * s, 0, [(0, 1), (0, -1)])
            for part in (0, 1):
                go(part, 0, s, [(0, s)])
        elif level == 3:
            for first in (s, -s, 2 * s):
                for part in (0, 1):
                    go(part, first, s, [(0, s)])
        else:
            for first in (0, s, -s, 2 * s):
                for part in (0, 1):
                    go(part, first, -s, [])
            for first in (0, s, -s, 2 * s):
                for part in (0, 1):
                    go(part, first, 2 * s, [])

    def from_sibling(ref, sem):
        arrived(ref, sem)

    here = x * ny + y
    z_first()
    xy_first(i_ref, i_cols, i_sem)
    kept = [
        keep(a_ref.at[c], x_rows.at[z, c], 0),
        keep(i_ref.at[c], i_cols.at[here, c], 1),
        keep(a_ref.at[c], a_cols.at[here, c], 2),
    ]
    z_step(1)
    xy_level(i_cols, i_sem, 1)
    z_step(2)
    xy_level(i_cols, i_sem, 2)
    z_step(3)
    xy_level(i_cols, i_sem, 3)
    xy_first(a_ref, a_cols, a_sem)
    z_step(4) if nz // 2 == 4 else None
    xy_level(i_cols, i_sem, 4)
    from_sibling(x_rows.at[z, 1 - c], x_sem.at[1 - c, z])
    from_sibling(i_cols.at[here, 1 - c], i_sem.at[1 - c, here])
    for copy in kept:
        copy.wait()

    def block(buf, k):
        return buf[2 * k : 2 * k + 2].reshape(width, width)

    total[...] = i_cols[here].reshape(2 * rows, width)
    for k in range(nz):
        total[...] += product(x_rows[k].reshape(2 * rows, width), block(i_cols, k))
        if k == 3:
            xy_level(a_cols, a_sem, 1)
    t_rows[z] = total[...]

    def t_slot(dz):
        at = lax.rem(z - dz + nz, nz)
        return t_rows.at[at], t_sem.at[at]

    slot, sem = t_slot(0)
    send(slot, slot, sem, device(0, 0, s, c))
    send(slot, slot, sem, device(0, 0, -s, c))
    xy_level(a_cols, a_sem, 2)
    for k in range(1, nz // 2 + 1):
        slot, sem = t_slot(s * k)
        arrived(slot, sem)
        if k < nz // 2:
            send(slot, slot, sem, device(0, 0, s, c))
            slot, sem = t_slot(-s * k)
            arrived(slot, sem)
            if k + 1 < nz // 2:
                send(slot, slot, sem, device(0, 0, -s, c))
        if k == 1:
            xy_level(a_cols, a_sem, 3)
    xy_level(a_cols, a_sem, 4)
    from_sibling(a_cols.at[here, 1 - c], a_sem.at[1 - c, here])

    for k in range(nz):
        total[...] += product(t_rows[k], block(a_cols, k))
    part = pl.ds(pl.multiple_of((1 - c) * rows, rows), rows)
    send(total.at[part], theirs, r_sem, device(0, 0, 0, 1 - c))
    o_ref[c] = total[pl.ds(pl.multiple_of(c * rows, rows), rows), :]
    arrived(theirs, r_sem)
    o_ref[1 - c] = theirs[...]
    for copy in started:
        copy.wait_send()


def shards(amplitudes, integrals, nx, ny, nz):
    classes, rows, width = amplitudes.shape
    f32 = jnp.float32
    dma = pltpu.SemaphoreType.DMA
    return pl.pallas_call(
        functools.partial(kernel, nx, ny, nz),
        out_shape=jax.ShapeDtypeStruct(amplitudes.shape, f32),
        in_specs=[pl.BlockSpec(memory_space=pltpu.VMEM)] * 2,
        out_specs=pl.BlockSpec(memory_space=pltpu.VMEM),
        scratch_shapes=[
            pltpu.VMEM((nz, 2, rows, width), f32),
            pltpu.VMEM((nx * ny, 2, rows, width), f32),
            pltpu.VMEM((nx * ny, 2, rows, width), f32),
            pltpu.VMEM((nz, 2 * rows, width), f32),
            pltpu.VMEM((2 * rows, width), f32),
            pltpu.VMEM((rows, width), f32),
            dma((128,)),
            dma((3,)),
            dma((2, nz)),
            dma((2, nx * ny)),
            dma((2, nx * ny)),
            dma((nz,)),
            dma,
        ],
        compiler_params=pltpu.CompilerParams(
            collective_id=0, has_side_effects=True, vmem_limit_bytes=40 * 1024 * 1024
        ),
    )(amplitudes, integrals)


def solution(mesh):
    nz = mesh.shape["int"]
    nx = ny = 4
    placed = P(None, "pair", "int")
    return jax.shard_map(
        functools.partial(shards, nx=nx, ny=ny, nz=nz),
        mesh=mesh, in_specs=(placed, placed), out_specs=placed, check_vma=False,
    )
```

time: 283 us -> 85.5 us (0.30)
  waiting for transfers between devices: 243 us -> 0 us
  Pallas kernels: 0 us -> 82.7 us
  matrix products: 24.3 us -> 0 us
  between operations: 13.1 us -> 0.01 us
    reduce_scatter x2 -> x0, waiting for transfers between devices: 148 us -> none  [the longest x1 105 us: shards(): lax.psum_scatter(jnp.einsum('hak,hkb->bha', cycle_inter, row_block, preci...]
    all_gather x2 -> x0, waiting for transfers between devices: 93.4 us -> none  [the longest x1 66.6 us: shards(): lax.all_gather(amplitudes, 'pair', axis=1, tiled=True)]
    pallas_call x0 -> x1, Pallas kernels: none -> 82.7 us  [shards(): pl.pallas_call(functools.partial(kernel, nx, ny, nz), out_shape=jax.Shape...]
    dot_general x2 -> x0, matrix products: 24.3 us -> none  [the longest x1 12.8 us: shards(): jnp.einsum('hkl,hbl->hkb', lax.all_gather(amplitudes, 'pair', axis=1, til...]
  transfers between devices with their start and end apart: 4 -> 0, of which waited for: 4 -> 0; matrix products, arithmetic and copies ran while one was open for 5% -> 0% of each run, Pallas kernels for 0% -> 0%
where the time goes in v1:
time: 85.5 us; the launch traced here: 85.4 us
  Pallas kernels  82.7 us (97%)
  local copies, waits for them, and re-layouts  2.64 us (3%)
    pallas_call x1, Pallas kernels, shards(): pl.pallas_call(functools.partial(kernel, nx, ny, nz), out_shape=jax.Shape...  82.7 us
    unnamed x5, local copies, waits for them, and re-layouts  2.64 us

profile of v1, /device:TPU:1, one launch (start us, length us, event | category | flops | bytes accessed | tf_op | source)
XLA Modules:
  0.0 85.4 jit_solution(3298268057553920131)
XLA Ops:
  0.0 0.0 copy-start
  0.0 1.0 %copy-done = f32[2,96,384]{2,1,0:T(8,128)S(1)} copy-done((f32[2,96,384]{2,1,0:T(8,128)S(1)}, f32[2,96,384]{2,1,0:T(8,128)}, u32[]{:S(2)}) %copy-start) | copy-done | bytes 294936
  1.0 0.0 copy-start.1
  1.0 1.0 %copy-done.1 = f32[2,96,384]{2,1,0:T(8,128)S(1)} copy-done((f32[2,96,384]{2,1,0:T(8,128)S(1)}, f32[2,96,384]{2,1,0:T(8,128)}, u32[]{:S(2)}) %copy-start.1) | copy-done | bytes 294936
  1.9 82.7 %shard_map.28 = f32[2,96,384]{2,1,0:T(8,128)S(1)} custom-call(f32[2,96,384]{2,1,0:T(8,128)S(1)} %copy-done, f32[2,96,384]{2,1,0:T(8,128)S(1)} %copy-done.1), custom_call_target="tpu_custom_call" | custom-call | tf_op jit(solution)/shard_map/pallas_call | solution.py:218
  84.7 0.7 copy.4
Async XLA Ops:
  0.0 1.0 %copy-start = (f32[2,96,384]{2,1,0:T(8,128)S(1)}, f32[2,96,384]{2,1,0:T(8,128)}, u32[]{:S(2)}) copy-start(f32[2,96,384]{2,1,0:T(8,128)} %a_ref.1) | copy-start | bytes 884740
  1.0 1.0 %copy-start.1 = (f32[2,96,384]{2,1,0:T(8,128)S(1)}, f32[2,96,384]{2,1,0:T(8,128)}, u32[]{:S(2)}) copy-start(f32[2,96,384]{2,1,0:T(8,128)} %i_ref.1) | copy-start | bytes 884740

commit v2 on v0

v2 whole, which is shorter than its diff:
```python
import functools

import jax
import jax.numpy as jnp
from jax import lax
from jax.experimental import pallas as pl
from jax.experimental.pallas import tpu as pltpu
from jax.sharding import PartitionSpec as P

MESH = pl.DeviceIdType.MESH
PARTS = 3


def split(v):
    high = v.astype(jnp.bfloat16)
    return high, (v - high.astype(jnp.float32)).astype(jnp.bfloat16)


def dot(a, b, transposed):
    dims = (((1,), (1 if transposed else 0,)), ((), ()))
    return lax.dot_general(a, b, dims, preferred_element_type=jnp.float32)


def product(a, b, transposed=False):
    go = functools.partial(dot, transposed=transposed)
    return go(a[0], b[0]) + (go(a[0], b[1]) + go(a[1], b[0]))


def xor(a, b):
    return a + b - 2 * a * b


def kernel(
    nx, ny, nz, a_ref, i_ref, o_ref,
    own, x_rows, i_all, t_part, t_all, x_high, x_low, i_high, i_low, r_part,
    send_sem, local_sem, x_sem, z_sem, i_sem, ta_sem, tg_sem, r_sem,
):
    width = i_ref.shape[2]
    pair, z = lax.axis_index("pair"), lax.axis_index("int")
    c = lax.rem(pair, 2)
    chip = pair // 2
    y, x = lax.rem(chip, ny), chip // ny
    s = 1 - 2 * c
    odd, half = lax.rem(y, 2), y // 2
    mine = odd

    def device(xx, yy, zz, core):
        return {"pair": (xx * ny + yy) * 2 + core, "int": zz}

    def xs(d):
        return lax.rem(x + d + nx, nx)

    def zs(d):
        return lax.rem(z + d + nz, nz)

    to_half, to_core = xor(half, odd), xor(c, 1 - odd)
    spread = [(h, k, device(k, 2 * to_half + h, z, to_core)) for h in (0, 1) for k in range(nx)]

    def source(xr, hr):
        o = xor(half, hr)
        return device(xr, 2 * hr + o, z, xor(c, 1 - o))

    sources = [source(xr, hr) for xr in range(nx) for hr in (0, 1)]

    def place(xx, hh, core, plane):
        o = xor(hh, plane % 2)
        return (o * 2 + xor(core, 1 - o)) * nx + xx

    started = []

    def send(src, dst, sem, to):
        copy = pltpu.make_async_remote_copy(
            src_ref=src, dst_ref=dst, send_sem=send_sem.at[len(started)], recv_sem=sem,
            device_id=to, device_id_type=MESH,
        )
        copy.start()
        started.append(copy)

    sibling = device(x, y, z, 1 - c)
    right, left = device(xs(1), y, z, c), device(xs(-1), y, z, c)
    ahead = device(xs(s), y, z, c)
    across = device(x, lax.rem(y + 2, ny), z, c)

    def arrived(ref, sem):
        pltpu.make_async_remote_copy(
            src_ref=ref, dst_ref=ref, send_sem=send_sem.at[0], recv_sem=sem,
            device_id=sibling, device_id_type=MESH,
        ).wait_recv()

    shape = a_ref.shape[1:]
    row = (
        24 * lax.broadcasted_iota(jnp.int32, shape, 0)
        + 8 * lax.broadcasted_iota(jnp.int32, shape, 1)
        + lax.broadcasted_iota(jnp.int32, shape, 2)
    )
    shift = jnp.where(x * 2 + half == z, (odd * 2 + c) * 24 * nx, -2 * width)
    ones = jnp.where(lax.broadcasted_iota(jnp.int32, shape, 3) == row + shift, 1.0, 0.0)
    for h in (0, 1):
        own[h] = a_ref[h] + ones

    barrier = pltpu.get_barrier_semaphore()
    peers = [to for _, _, to in spread] + sources
    peers += [device(x, yy, z, 1 - c) for yy in range(ny)]
    peers += [right, left, across] + [device(x, y, zs(d), c) for d in range(1, nz)]
    for peer in peers:
        pl.semaphore_signal(barrier, inc=1, device_id=peer, device_id_type=MESH)
    pl.semaphore_wait(barrier, len(peers))

    block = x * 2 + half
    for h, k, to in spread:
        send(own.at[h, k], x_rows.at[z, :, block], x_sem.at[block], to)
    for h in (0, 1):
        for hh in (0, 1):
            send(i_ref.at[h], i_all.at[x, y, c], i_sem.at[x, y, c], device(x, 2 * hh + h, z, 1 - c))

    def z_slot(d, g):
        at = zs(-d)
        return x_rows.at[at, g], z_sem.at[at, g]

    def z_own(g):
        slot, sem = z_slot(0, g)
        send(slot, slot, sem, device(x, y, zs(s), c))
        send(slot, slot, sem, device(x, y, zs(-s), c))

    far = nz // 2

    def z_step(k, g):
        slot, sem = z_slot(s * k, g)
        arrived(slot, sem)
        if k < far:
            send(slot, slot, sem, device(x, y, zs(s), c))
            slot, sem = z_slot(-s * k, g)
            arrived(slot, sem)
            if k + 1 < far:
                send(slot, slot, sem, device(x, y, zs(-s), c))

    def i_slot(d, yy, core):
        at = xs(-d)
        return i_all.at[at, yy, core], i_sem.at[at, yy, core]

    def i_step(d, yy):
        slot, sem = i_slot(s * d, yy, 1 - c)
        arrived(slot, sem)
        if d == 0:
            send(slot, slot, sem, right)
            send(slot, slot, sem, left)
        elif d == 1:
            send(slot, slot, sem, ahead)
        send(slot, slot, sem, sibling)

    for r in range(nx * 2):
        arrived(x_rows.at[z, :, r], x_sem.at[r])
    z_own(0)
    z_own(1)
    for yy in range(ny):
        i_step(0, yy)
    z_step(1, 0)
    z_own(2)
    i_step(1, 0)
    i_step(1, 1)
    z_step(1, 1)
    z_step(2, 0)
    i_step(1, 2)
    i_step(1, 3)
    z_step(1, 2)
    i_step(-1, 0)
    i_step(-1, 1)
    z_step(2, 1)
    z_step(3, 0)
    i_step(-1, 2)
    i_step(-1, 3)
    z_step(2, 2)
    i_step(2, 0)
    i_step(2, 1)
    z_step(3, 1)
    z_step(4, 0)
    i_step(2, 2)
    i_step(2, 3)
    for d in (0, 1, -1, 2):
        for yy in range(ny):
            arrived(*i_slot(s * d, yy, c))

    def i_split(k):
        v = i_all[k // 2, 2 * (k % 2) : 2 * (k % 2) + 2].reshape(width, width)
        i_high[k], i_low[k] = split(v)

    rows_of = 8 * nz

    def t_product(g):
        total = jnp.zeros((rows_of, width), jnp.float32)
        at = pl.ds(g * rows_of, rows_of)
        for k in range(nz):
            high, low = split(x_rows[k, g].reshape(rows_of, width))
            x_high[k, at], x_low[k, at] = high, low
            total += product((high, low), (i_high[k], i_low[k]))
        t_part[g] = total.reshape(nz, 8, width)

    kept = []

    def t_spread(g):
        for d in (0, 1, -1, 2, -2, 3, -3, 4):
            to = zs(d)
            dst = t_all.at[z, place(x, half, c, to), g]
            if d == 0:
                copy = pltpu.make_async_copy(t_part.at[g, to], dst, local_sem.at[g])
                copy.start()
                kept.append(copy)
            else:
                send(t_part.at[g, to], dst, ta_sem.at[z, g], device(x, y, to, c))

    here = place(x, half, c, z)

    def t_own(g):
        kept[g].wait()
        for d in range(1, nz):
            at = zs(d)
            arrived(t_all.at[at, here, g], ta_sem.at[at, g])
        slot, sem = t_all.at[:, here, g], tg_sem.at[here, g]
        for to in (across, right, left, sibling):
            send(slot, slot, sem, to)

    def t_step(d, other, g):
        at = place(xs(-s * d), xor(half, other), c, z)
        slot, sem = t_all.at[:, at, g], tg_sem.at[at, g]
        arrived(slot, sem)
        if d == 0:
            send(slot, slot, sem, right)
            send(slot, slot, sem, left)
        elif d == 1:
            send(slot, slot, sem, ahead)
        send(slot, slot, sem, sibling)

    for k in range(nz):
        i_split(k)
    t_product(0)
    t_spread(0)
    z_step(3, 2)
    z_step(4, 1)
    t_product(1)
    t_spread(1)
    t_own(0)
    z_step(4, 2)
    t_product(2)
    t_spread(2)
    t_step(0, 1, 0)
    t_step(1, 0, 0)
    t_own(1)
    t_step(1, 1, 0)
    t_step(0, 1, 1)
    t_own(2)
    t_step(1, 0, 1)
    t_step(1, 1, 1)
    t_step(0, 1, 2)
    t_step(1, 0, 2)
    t_step(1, 1, 2)
    for g in range(PARTS):
        for d in (-1, 2):
            for other in (0, 1):
                t_step(d, other, g)
    for g in range(PARTS):
        for d in (0, 1, -1, 2):
            for other in (0, 1):
                at = place(xs(-s * d), xor(half, other), 1 - c, z)
                arrived(t_all.at[:, at, g], tg_sem.at[at, g])

    total = jnp.zeros((PARTS * rows_of, width), jnp.float32)
    for k in range(nz):
        t = split(t_all[k].reshape(width, width))
        total += product((x_high[k], x_low[k]), t, transposed=True)
    r_part[...] = total.reshape(r_part.shape)
    for k, to in enumerate(sources):
        send(r_part.at[:, k], o_ref.at[mine, x], r_sem.at[mine, x], to)
    for h in (0, 1):
        for k in range(nx):
            arrived(o_ref.at[h, k], r_sem.at[h, k])
    for copy in started:
        copy.wait_send()


def shards(amplitudes, integrals, nx, ny, nz):
    classes, rows, width = amplitudes.shape
    f32, b16 = jnp.float32, jnp.bfloat16
    dma = pltpu.SemaphoreType.DMA
    cut = (classes, nx, PARTS, 8, width)
    out = pl.pallas_call(
        functools.partial(kernel, nx, ny, nz),
        out_shape=jax.ShapeDtypeStruct(cut, f32),
        in_specs=[pl.BlockSpec(memory_space=pltpu.VMEM)] * 2,
        out_specs=pl.BlockSpec(memory_space=pltpu.VMEM),
        scratch_shapes=[
            pltpu.VMEM(cut, f32),
            pltpu.VMEM((nz, PARTS, nz, 8, width), f32),
            pltpu.VMEM((nx, ny, 2, rows, width), f32),
            pltpu.VMEM((PARTS, nz, 8, width), f32),
            pltpu.VMEM((nz, 4 * nx, PARTS, 8, width), f32),
            pltpu.VMEM((nz, 2 * rows, width), b16),
            pltpu.VMEM((nz, 2 * rows, width), b16),
            pltpu.VMEM((nz, width, width), b16),
            pltpu.VMEM((nz, width, width), b16),
            pltpu.VMEM((PARTS, nz, 8, width), f32),
            dma((160,)),
            dma((PARTS,)),
            dma((nx * 2,)),
            dma((nz, PARTS)),
            dma((nx, ny, 2)),
            dma((nz, PARTS)),
            dma((4 * nx, PARTS)),
            dma((2, nx)),
        ],
        compiler_params=pltpu.CompilerParams(
            collective_id=0, has_side_effects=True, vmem_limit_bytes=48 * 1024 * 1024
        ),
    )(amplitudes.reshape(cut), integrals)
    return out.reshape(amplitudes.shape)


def solution(mesh):
    nz = mesh.shape["int"]
    nx = ny = 4
    placed = P(None, "pair", "int")
    return jax.shard_map(
        functools.partial(shards, nx=nx, ny=ny, nz=nz),
        mesh=mesh, in_specs=(placed, placed), out_specs=placed, check_vma=False,
    )
```

time: 283 us -> 93.3 us (0.33)
  the two profiles are of different devices: /device:TPU:1 before, /device:TPU:9 now
where the time goes in v2:
time: 93.3 us; the launch traced here: 93.2 us
  Pallas kernels  90.6 us (97%)
  local copies, waits for them, and re-layouts  2.64 us (3%)
    pallas_call x1, Pallas kernels, shards(): pl.pallas_call(functools.partial(kernel, nx, ny, nz), out_shape=jax.Shape...  90.6 us
    unnamed x5, local copies, waits for them, and re-layouts  2.64 us

profile of v2, /device:TPU:9, one launch (start us, length us, event | category | flops | bytes accessed | tf_op | source)
XLA Modules:
  0.0 93.2 jit_solution(18399549985392427533)
XLA Ops:
  0.0 0.0 copy-start
  0.0 1.0 %copy-done = f32[2,96,384]{2,1,0:T(8,128)S(1)} copy-done((f32[2,96,384]{2,1,0:T(8,128)S(1)}, f32[2,96,384]{2,1,0:T(8,128)}, u32[]{:S(2)}) %copy-start) | copy-done | bytes 294936
  1.0 0.0 copy-start.1
  1.0 1.0 %copy-done.1 = f32[2,96,384]{2,1,0:T(8,128)S(1)} copy-done((f32[2,96,384]{2,1,0:T(8,128)S(1)}, f32[2,96,384]{2,1,0:T(8,128)}, u32[]{:S(2)}) %copy-start.1) | copy-done | bytes 294936
  1.9 90.6 %shard_map.28 = f32[2,4,3,8,384]{4,3,2,1,0:T(8,128)S(1)} custom-call(f32[2,4,3,8,384]{4,3,2,1,0:T(8,128)S(1)} %bitcast.3, f32[2,96,384]{2,1,0:T(8,128)S(1)} %copy-done.1), custom_call_target="tpu_custom_call" | custom-call | tf_op jit(solution)/shard_map/pallas_call | solution.py:285
  92.5 0.7 copy.4
Async XLA Ops:
  0.0 1.0 %copy-start = (f32[2,96,384]{2,1,0:T(8,128)S(1)}, f32[2,96,384]{2,1,0:T(8,128)}, u32[]{:S(2)}) copy-start(f32[2,96,384]{2,1,0:T(8,128)} %param.2) | copy-start | bytes 884740
  1.0 1.0 %copy-start.1 = (f32[2,96,384]{2,1,0:T(8,128)S(1)}, f32[2,96,384]{2,1,0:T(8,128)}, u32[]{:S(2)}) copy-start(f32[2,96,384]{2,1,0:T(8,128)} %i_ref.1) | copy-start | bytes 884740

commit v3 on v2

v3 whole, which is shorter than its diff:
```python
import functools

import jax
import jax.numpy as jnp
from jax import lax
from jax.experimental import pallas as pl
from jax.experimental.pallas import tpu as pltpu
from jax.sharding import PartitionSpec as P

MESH = pl.DeviceIdType.MESH
PARTS = 3
X_FIRST = (0,)


def split(v):
    high = v.astype(jnp.bfloat16)
    return high, (v - high.astype(jnp.float32)).astype(jnp.bfloat16)


def dot(a, b, transposed):
    dims = (((1,), (1 if transposed else 0,)), ((), ()))
    return lax.dot_general(a, b, dims, preferred_element_type=jnp.float32)


def product(a, b, transposed=False):
    go = functools.partial(dot, transposed=transposed)
    return go(a[0], b[0]) + (go(a[0], b[1]) + go(a[1], b[0]))


def xor(a, b):
    return a + b - 2 * a * b


def kernel(
    nx, ny, nz, a_ref, i_ref, o_ref,
    own, x_rows, i_all, t_part, t_all, x_high, x_low, i_high, i_low, r_turned, r_part,
    send_sem, local_sem, x_sem, z_sem, i_sem, ta_sem, tg_sem, r_sem,
):
    width = i_ref.shape[2]
    pair, z = lax.axis_index("pair"), lax.axis_index("int")
    c = lax.rem(pair, 2)
    chip = pair // 2
    y, x = lax.rem(chip, ny), chip // ny
    s = 1 - 2 * c
    odd, mine = lax.rem(y, 2), y // 2

    def device(xx, yy, zz, core):
        return {"pair": (xx * ny + yy) * 2 + core, "int": zz}

    def xs(d):
        return lax.rem(x + d + nx, nx)

    def ys(d):
        return lax.rem(y + d, ny)

    def zs(d):
        return lax.rem(z + d + nz, nz)

    spread = [(h, k, device(k, 2 * h + odd, z, 1 - c)) for h in (0, 1) for k in range(nx)]
    sources = [device(xr, 2 * hr + odd, z, 1 - c) for xr in range(nx) for hr in (0, 1)]

    def place(xx, parity, core):
        return (parity * 2 + 1 - core) * nx + xx

    started = []

    def send(src, dst, sem, to):
        copy = pltpu.make_async_remote_copy(
            src_ref=src, dst_ref=dst, send_sem=send_sem.at[len(started)], recv_sem=sem,
            device_id=to, device_id_type=MESH,
        )
        copy.start()
        started.append(copy)

    sibling = device(x, y, z, 1 - c)
    right, left = device(xs(1), y, z, c), device(xs(-1), y, z, c)
    ahead = device(xs(s), y, z, c)
    across = device(x, 2 * mine + 1 - odd, z, c)

    def arrived(ref, sem):
        pltpu.make_async_remote_copy(
            src_ref=ref, dst_ref=ref, send_sem=send_sem.at[0], recv_sem=sem,
            device_id=sibling, device_id_type=MESH,
        ).wait_recv()

    fetch = pltpu.make_async_copy(a_ref, own, local_sem.at[PARTS])
    fetch.start()
    barrier = pltpu.get_barrier_semaphore()
    peers = [to for _, _, to in spread] + [device(x, ys(d), z, 1 - c) for d in (1, 3)]
    peers += [right, left, across] + [device(x, y, zs(d), c) for d in range(1, nz)]
    for peer in peers:
        pl.semaphore_signal(barrier, inc=1, device_id=peer, device_id_type=MESH)

    shape = own.shape[1:]
    row = (
        24 * lax.broadcasted_iota(jnp.int32, shape, 0)
        + 8 * lax.broadcasted_iota(jnp.int32, shape, 1)
        + lax.broadcasted_iota(jnp.int32, shape, 2)
    )
    block = x * 2 + mine
    shift = jnp.where(block == z, (odd * 2 + c) * 24 * nx, -2 * width)
    ones = jnp.where(lax.broadcasted_iota(jnp.int32, shape, 3) == row + shift, 1.0, 0.0)
    fetch.wait()
    for h in (0, 1):
        own[h] = own[h] + ones
    pl.semaphore_wait(barrier, len(peers))

    for h, k, to in spread:
        send(own.at[h, k], x_rows.at[z, :, block], x_sem.at[block], to)

    def i_first():
        for d in (0, 1, 3, 2):
            yy = ys(d)
            send(i_ref.at[yy // 2], i_all.at[x, y, c], i_sem.at[x, y, c], device(x, yy, z, 1 - c))

    def z_slot(d, g):
        at = zs(-d)
        return x_rows.at[at, g], z_sem.at[at, g]

    def z_own(g):
        slot, sem = z_slot(0, g)
        send(slot, slot, sem, device(x, y, zs(s), c))
        send(slot, slot, sem, device(x, y, zs(-s), c))

    far = nz // 2

    def z_step(k, g):
        slot, sem = z_slot(s * k, g)
        arrived(slot, sem)
        if k < far:
            send(slot, slot, sem, device(x, y, zs(s), c))
            slot, sem = z_slot(-s * k, g)
            arrived(slot, sem)
            if k + 1 < far:
                send(slot, slot, sem, device(x, y, zs(-s), c))

    def i_keep(at, yy, core):
        high, low = split(i_all[at, yy, core])
        i_high[at, yy, core] = high
        i_low[at, yy, core] = low

    def i_step(d, dy):
        at, yy = xs(-s * d), ys(dy)
        slot, sem = i_all.at[at, yy, 1 - c], i_sem.at[at, yy, 1 - c]
        arrived(slot, sem)
        if d == 0:
            send(slot, slot, sem, right)
            send(slot, slot, sem, left)
        elif d == 1:
            send(slot, slot, sem, ahead)
        send(slot, slot, sem, sibling)
        i_keep(at, yy, 1 - c)

    def i_shared(d, dy):
        at, yy = xs(-s * d), ys(dy)
        arrived(i_all.at[at, yy, c], i_sem.at[at, yy, c])
        i_keep(at, yy, c)

    rows_of = 8 * nz

    def t_product(g):
        total = jnp.zeros((rows_of, width), jnp.float32)
        at = pl.ds(g * rows_of, rows_of)
        for k in range(nz):
            high, low = split(x_rows[k, g].reshape(rows_of, width))
            x_high[k, at], x_low[k, at] = high, low
            where = (k // 2, slice(2 * (k % 2), 2 * (k % 2) + 2))
            total += product((high, low), [v[where].reshape(width, width) for v in (i_high, i_low)])
        t_part[g] = total.reshape(nz, 8, width)

    kept = []
    here = place(x, odd, c)

    def t_spread(g):
        dst = t_all.at[g, z, here]
        copy = pltpu.make_async_copy(t_part.at[g, z], dst, local_sem.at[g])
        copy.start()
        kept.append(copy)
        for d in (1, -1, 2, -2, 3, -3, 4):
            to = zs(d)
            send(t_part.at[g, to], dst, ta_sem.at[z, g], device(x, y, to, c))

    def t_slot(d, other, core, g):
        at = place(xs(-s * d), xor(odd, other), core)
        return t_all.at[g, :, at], tg_sem.at[at, g]

    def t_own(g):
        kept[g].wait()
        for d in (1, -1, 2, -2, 3, -3, 4):
            at = zs(d)
            arrived(t_all.at[g, at, here], ta_sem.at[at, g])
        slot, sem = t_slot(0, 0, c, g)
        for to in (right, left, across, sibling):
            send(slot, slot, sem, to)

    def t_step(d, other, g):
        slot, sem = t_slot(d, other, c, g)
        arrived(slot, sem)
        if g in X_FIRST:
            if other == 0:
                if d == 1:
                    send(slot, slot, sem, ahead)
                send(slot, slot, sem, across)
        elif d == 0:
            send(slot, slot, sem, right)
            send(slot, slot, sem, left)
        elif d == 1:
            send(slot, slot, sem, ahead)
        send(slot, slot, sem, sibling)

    def t_shared(g):
        for d in (0, 1, -1, 2):
            for other in (0, 1):
                arrived(*t_slot(d, other, 1 - c, g))

    def r_product(g):
        total = jnp.zeros((16 * nz, PARTS * rows_of), jnp.float32)
        for k in range(nz):
            t = split(t_all[g, k].reshape(16 * nz, width))
            total += product(t, (x_high[k], x_low[k]), transposed=True)
        r_turned[:, g] = total.reshape(4 * nx, 8, PARTS * rows_of)

    for r in range(nx * 2):
        arrived(x_rows.at[z, :, r], x_sem.at[r])
    z_own(0)
    z_own(1)
    i_first()
    i_step(0, 0)
    z_step(1, 0)
    z_own(2)
    i_step(0, 1)
    i_step(0, 3)
    z_step(1, 1)
    i_step(1, 0)
    z_step(2, 0)
    i_step(0, 2)
    i_step(-1, 0)
    z_step(1, 2)
    i_step(1, 1)
    i_step(1, 3)
    z_step(2, 1)
    z_step(3, 0)
    i_step(2, 0)
    i_step(-1, 1)
    i_step(-1, 3)
    z_step(2, 2)
    i_step(1, 2)
    i_step(2, 1)
    z_step(3, 1)
    z_step(4, 0)
    i_step(2, 3)
    for d in (0, 1, -1):
        for dy in (0, 1, 3):
            i_shared(d, dy)
    z_step(3, 2)
    i_step(-1, 2)
    i_step(2, 2)
    for d, dy in ((0, 2), (1, 2), (2, 0), (2, 1), (2, 3), (-1, 2), (2, 2)):
        i_shared(d, dy)
    t_product(0)
    t_spread(0)
    z_step(4, 1)
    t_product(1)
    t_spread(1)
    t_own(0)
    z_step(4, 2)
    t_product(2)
    t_spread(2)
    t_step(1, 0, 0)
    t_step(-1, 0, 0)
    t_own(1)
    t_step(0, 1, 0)
    t_step(2, 0, 0)
    t_own(2)
    t_step(0, 1, 1)
    t_step(1, 0, 1)
    t_step(1, 1, 0)
    t_step(-1, 1, 0)
    t_step(1, 1, 1)
    t_step(0, 1, 2)
    t_step(1, 0, 2)
    t_step(2, 1, 0)
    t_shared(0)
    r_product(0)
    for d in (-1, 2):
        for other in (0, 1):
            t_step(d, other, 1)
    t_step(1, 1, 2)
    t_shared(1)
    r_product(1)
    for d in (-1, 2):
        for other in (0, 1):
            t_step(d, other, 2)
    t_shared(2)
    r_product(2)
    turned = r_turned[...].reshape(width, PARTS * rows_of)
    r_part[...] = jnp.transpose(turned).reshape(r_part.shape)
    for k, to in enumerate(sources):
        send(r_part.at[:, k], o_ref.at[mine, x], r_sem.at[mine, x], to)
    for h in (0, 1):
        for k in range(nx):
            arrived(o_ref.at[h, k], r_sem.at[h, k])
    for copy in started:
        copy.wait_send()


def shards(amplitudes, integrals, nx, ny, nz):
    classes, rows, width = amplitudes.shape
    f32, b16 = jnp.float32, jnp.bfloat16
    dma = pltpu.SemaphoreType.DMA
    cut = (classes, nx, PARTS, 8, width)
    out = pl.pallas_call(
        functools.partial(kernel, nx, ny, nz),
        out_shape=jax.ShapeDtypeStruct(cut, f32),
        in_specs=[pl.BlockSpec(memory_space=pl.ANY)] * 2,
        out_specs=pl.BlockSpec(memory_space=pltpu.VMEM),
        scratch_shapes=[
            pltpu.VMEM(cut, f32),
            pltpu.VMEM((nz, PARTS, nz, 8, width), f32),
            pltpu.VMEM((nx, ny, 2, rows, width), f32),
            pltpu.VMEM((PARTS, nz, 8, width), f32),
            pltpu.VMEM((PARTS, nz, 4 * nx, 8, width), f32),
            pltpu.VMEM((nz, 2 * rows, width), b16),
            pltpu.VMEM((nz, 2 * rows, width), b16),
            pltpu.VMEM((nx, ny, 2, rows, width), b16),
            pltpu.VMEM((nx, ny, 2, rows, width), b16),
            pltpu.VMEM((4 * nx, PARTS, 8, PARTS * 8 * nz), f32),
            pltpu.VMEM((PARTS, nz, 8, width), f32),
            dma((160,)),
            dma((PARTS + 1,)),
            dma((nx * 2,)),
            dma((nz, PARTS)),
            dma((nx, ny, 2)),
            dma((nz, PARTS)),
            dma((4 * nx, PARTS)),
            dma((2, nx)),
        ],
        compiler_params=pltpu.CompilerParams(
            collective_id=0, has_side_effects=True, vmem_limit_bytes=56 * 1024 * 1024
        ),
    )(amplitudes.reshape(cut), integrals)
    return out.reshape(amplitudes.shape)


def solution(mesh):
    nz = mesh.shape["int"]
    nx = ny = 4
    placed = P(None, "pair", "int")
    return jax.shard_map(
        functools.partial(shards, nx=nx, ny=ny, nz=nz),
        mesh=mesh, in_specs=(placed, placed), out_specs=placed, check_vma=False,
    )
```

time: 93.3 us -> 89.7 us (0.961)
  the two profiles are of different devices: /device:TPU:9 before, /device:TPU:1 now
where the time goes in v3:
time: 89.7 us; the launch traced here: 89.5 us
  Pallas kernels  87.8 us (98%)
  local copies, waits for them, and re-layouts  1.7 us (2%)
    pallas_call x1, Pallas kernels, shards(): pl.pallas_call(functools.partial(kernel, nx, ny, nz), out_shape=jax.Shape...  87.8 us

profile of v3, /device:TPU:1, one launch (start us, length us, event | category | flops | bytes accessed | tf_op | source)
XLA Modules:
  0.0 89.5 jit_solution(5952714534945658681)
XLA Ops:
  0.0 87.8 %shard_map.28 = f32[2,4,3,8,384]{4,3,2,1,0:T(8,128)} custom-call(f32[2,4,3,8,384]{4,3,2,1,0:T(8,128)} %bitcast.3, f32[2,96,384]{2,1,0:T(8,128)} %i_ref.1), custom_call_target="tpu_custom_call" | custom-call | tf_op jit(solution)/shard_map/pallas_call | solution.py:312
  87.8 1.7 %copy.4 = f32[2,96,384]{2,1,0:T(8,128)} copy(f32[2,96,384]{2,1,0:T(8,128)} %bitcast.2) | data formatting | bytes 589824

commit v4 on v0

v4 whole, which is shorter than its diff:
```python
import functools

import jax
import jax.numpy as jnp
from jax import lax
from jax.experimental import pallas as pl
from jax.experimental.pallas import tpu as pltpu
from jax.sharding import PartitionSpec as P

MESH = pl.DeviceIdType.MESH
ORDER = (
    ("X", 1, 0), ("I", 1, 0, 0), ("X", 0, 1), ("I", 0, -1, 0), ("I", 0, 1, 0), ("X", 0, -1),
    ("I", 0, 0, 1), ("I", 0, 0, -1), ("X", 1, 1), ("X", 1, -1), ("I", 1, 0, -1), ("I", 1, 1, 0),
    ("I", 1, -1, 0), ("X", 0, -2), ("I", 1, 0, 1), ("I", 0, 2, 0), ("X", 0, 2), ("I", 0, -1, 1),
    ("I", 0, -1, -1), ("I", 0, 1, -1), ("I", 0, 1, 1), ("I", 0, 0, 2), ("X", 1, 2), ("X", 1, -2),
    ("I", 1, 1, 1), ("I", 1, -1, 1), ("X", 0, -3), ("X", 0, 3), ("I", 1, 1, -1), ("I", 1, 0, 2),
    ("I", 1, 2, 0), ("I", 1, -1, -1), ("I", 1, 1, 2), ("X", 1, 3), ("I", 0, 2, 1), ("X", 1, -3),
    ("I", 1, -1, 2), ("I", 0, 2, -1), ("X", 0, 4), ("I", 1, 2, -1), ("I", 1, 2, 1), ("I", 0, -1, 2),
    ("own",), ("X", 1, 4), ("I", 0, 1, 2), ("I", 1, 2, 2), ("I", 0, 2, 2), ("comp", 1),
    ("A", 0, -1, 0), ("A", 0, 1, 0), ("A", 0, 0, 1), ("A", 0, 0, -1), ("A", 1, 0, 0), ("comp", 0),
    ("T", 1, 1), ("T", 1, -1), ("A", 1, 0, 1), ("A", 1, 1, 0), ("A", 1, -1, 0), ("A", 1, 0, -1),
    ("A", 0, 2, 0), ("T", 0, -1), ("T", 0, 1), ("A", 0, -1, 1), ("A", 0, -1, -1), ("A", 0, 1, -1),
    ("A", 0, 1, 1), ("A", 1, 0, 2), ("T", 1, -2), ("T", 1, 2), ("A", 0, 0, 2), ("A", 1, 1, -1),
    ("T", 0, -2), ("T", 0, 2), ("A", 1, 1, 1), ("A", 1, 2, 0), ("A", 1, -1, 1), ("A", 1, -1, -1),
    ("T", 1, 3), ("T", 1, -3), ("A", 0, 2, 1), ("A", 0, 2, -1), ("A", 1, 1, 2), ("A", 0, -1, 2),
    ("A", 1, 2, 1), ("T", 0, -3), ("T", 0, 3), ("A", 1, 2, -1), ("A", 1, -1, 2), ("A", 0, 1, 2),
    ("A", 1, 2, 2), ("T", 1, 4), ("A", 0, 2, 2), ("R", 1), ("R", -3), ("R", 2), ("R", -2), ("R", 0),
    ("R", -1), ("R", 3), ("T", 0, 4), ("R", 4),
)


def split(v):
    high = v.astype(jnp.bfloat16)
    return high, (v - high.astype(jnp.float32)).astype(jnp.bfloat16)


def product(a, b):
    dot = functools.partial(jnp.dot, preferred_element_type=jnp.float32)
    return dot(a[0], b[0]) + (dot(a[0], b[1]) + dot(a[1], b[0]))


def kernel(
    nx, ny, nz, a_ref, i_ref, o_ref,
    x_rows, i_cols, a_cols, t_rows, total, theirs,
    x_high, x_low, i_high, i_low, a_high, a_low, t_high, t_low,
    send_sem, x_sem, i_sem, a_sem, t_sem, r_sem,
):
    rows = a_ref.shape[1]
    width = a_ref.shape[2]
    pair, z = lax.axis_index("pair"), lax.axis_index("int")
    c = lax.rem(pair, 2)
    chip = pair // 2
    y, x = lax.rem(chip, ny), chip // ny
    here = chip
    s = 1 - 2 * c
    parts = (c, 1 - c)

    def device(dx, dy, dz, core):
        xx, yy = lax.rem(x + dx + nx, nx), lax.rem(y + dy + ny, ny)
        zz = lax.rem(z + dz + nz, nz)
        return {"pair": (xx * ny + yy) * 2 + core, "int": zz}

    sibling = device(0, 0, 0, 1 - c)
    peers = [sibling]
    for core in (0, 1):
        for d in (1, -1):
            peers += [device(d, 0, 0, core), device(0, d, 0, core), device(0, 0, d, core)]
    barrier = pltpu.get_barrier_semaphore()
    for peer in peers:
        pl.semaphore_signal(barrier, inc=1, device_id=peer, device_id_type=MESH)
    pl.semaphore_wait(barrier, len(peers))

    started = []

    def send(src, dst, sem, to):
        copy = pltpu.make_async_remote_copy(
            src_ref=src, dst_ref=dst, send_sem=send_sem.at[len(started)], recv_sem=sem,
            device_id=to, device_id_type=MESH,
        )
        copy.start()
        started.append(copy)

    def arrived(ref, sem):
        pltpu.make_async_remote_copy(
            src_ref=ref, dst_ref=ref, send_sem=send_sem.at[0], recv_sem=sem,
            device_id=sibling, device_id_type=MESH,
        ).wait_recv()

    def keep(v, high, low, at, part):
        high[at, part], low[at, part] = split(v)

    def zs(d):
        return lax.rem(z + d + nz, nz)

    far = nz // 2

    def z_first():
        slot, sem = x_rows.at[z, c], x_sem.at[c, z]
        for d in (s, -s):
            for h in (c, 1 - c):
                send(a_ref.at[h], slot, sem, device(0, 0, d, h))
        send(a_ref.at[1 - c], slot, sem, sibling)
        keep(a_ref[c], x_high, x_low, z, c)

    def z_event(buf, sems, high, low, own, k):
        at, part = zs(-s * k), parts[own]
        slot, sem = buf.at[at, part], sems.at[part, at]
        arrived(slot, sem)
        if 0 < k < far:
            send(slot, slot, sem, device(0, 0, s, c))
        elif 1 - far < k < 0:
            send(slot, slot, sem, device(0, 0, -s, c))
        keep(buf[at, part], high, low, at, part)

    def turn(part, first, second):
        return first * (1 - part) + second * part, first * part + second * (1 - part)

    def xy_own(ref, buf, sems, high, low):
        slot, sem = buf.at[here, c], sems.at[c, here]

        def out(first, second):
            dx, dy = turn(c, first, second)
            for h in (c, 1 - c):
                send(ref.at[h], slot, sem, device(dx, dy, 0, h))

        out(s, 0)
        out(-s, 0)
        send(ref.at[1 - c], slot, sem, sibling)
        out(0, s)
        out(0, -s)
        keep(ref[c], high, low, here, c)

    def xy_event(buf, sems, high, low, own, first, second):
        part = parts[own]
        dx, dy = turn(part, s * first, s * second)
        at = lax.rem(x - dx + nx, nx) * ny + lax.rem(y - dy + ny, ny)
        slot, sem = buf.at[at, part], sems.at[part, at]
        arrived(slot, sem)
        along = []
        if second == 0 and first != 0:
            along = [(s, 0)] if first == 1 else []
            along += [(0, s), (0, -s)]
        elif second == 1:
            along = [(0, s)]
        for f, g in along:
            dx, dy = turn(part, f, g)
            send(slot, slot, sem, device(dx, dy, 0, c))
        keep(buf[at, part], high, low, at, part)

    def block(buf, k):
        return buf[pl.ds(2 * k, 2)].reshape(width, width)

    def t_event(own):
        part = parts[own]
        at = pl.ds(pl.multiple_of(part * rows, rows), rows)
        value = i_ref[c] if own == 0 else i_cols[here, part]
        for k in range(nz):
            value += product(
                (x_high[k, part], x_low[k, part]), (block(i_high, k), block(i_low, k))
            )
        total[at, :] = value
        t_rows[z, part] = value
        slot, sem = t_rows.at[z, part], t_sem.at[part, z]
        send(slot, slot, sem, device(0, 0, s, c))
        send(slot, slot, sem, device(0, 0, -s, c))
        keep(value, t_high, t_low, z, part)

    def r_event(k):
        at = zs(-s * k)
        t = [v[at].reshape(2 * rows, width) for v in (t_high, t_low)]
        total[...] += product(t, (block(a_high, at), block(a_low, at)))

    z_first()
    xy_own(i_ref, i_cols, i_sem, i_high, i_low)
    for name, *what in ORDER:
        if name == "X":
            z_event(x_rows, x_sem, x_high, x_low, *what)
        elif name == "T":
            z_event(t_rows, t_sem, t_high, t_low, *what)
        elif name == "I":
            xy_event(i_cols, i_sem, i_high, i_low, *what)
        elif name == "A":
            xy_event(a_cols, a_sem, a_high, a_low, *what)
        elif name == "own":
            xy_own(a_ref, a_cols, a_sem, a_high, a_low)
        elif name == "comp":
            t_event(*what)
        else:
            r_event(*what)
    part = pl.ds(pl.multiple_of((1 - c) * rows, rows), rows)
    send(total.at[part], theirs, r_sem, sibling)
    o_ref[c] = total[pl.ds(pl.multiple_of(c * rows, rows), rows), :]
    arrived(theirs, r_sem)
    o_ref[1 - c] = theirs[...]
    for copy in started:
        copy.wait_send()


def shards(amplitudes, integrals, nx, ny, nz):
    classes, rows, width = amplitudes.shape
    f32, b16 = jnp.float32, jnp.bfloat16
    dma = pltpu.SemaphoreType.DMA
    return pl.pallas_call(
        functools.partial(kernel, nx, ny, nz),
        out_shape=jax.ShapeDtypeStruct(amplitudes.shape, f32),
        in_specs=[pl.BlockSpec(memory_space=pltpu.VMEM)] * 2,
        out_specs=pl.BlockSpec(memory_space=pltpu.VMEM),
        scratch_shapes=[
            pltpu.VMEM((nz, 2, rows, width), f32),
            pltpu.VMEM((nx * ny, 2, rows, width), f32),
            pltpu.VMEM((nx * ny, 2, rows, width), f32),
            pltpu.VMEM((nz, 2, rows, width), f32),
            pltpu.VMEM((2 * rows, width), f32),
            pltpu.VMEM((rows, width), f32),
            pltpu.VMEM((nz, 2, rows, width), b16),
            pltpu.VMEM((nz, 2, rows, width), b16),
            pltpu.VMEM((nx * ny, 2, rows, width), b16),
            pltpu.VMEM((nx * ny, 2, rows, width), b16),
            pltpu.VMEM((nx * ny, 2, rows, width), b16),
            pltpu.VMEM((nx * ny, 2, rows, width), b16),
            pltpu.VMEM((nz, 2, rows, width), b16),
            pltpu.VMEM((nz, 2, rows, width), b16),
            dma((128,)),
            dma((2, nz)),
            dma((2, nx * ny)),
            dma((2, nx * ny)),
            dma((2, nz)),
            dma,
        ],
        compiler_params=pltpu.CompilerParams(
            collective_id=0, has_side_effects=True, vmem_limit_bytes=48 * 1024 * 1024
        ),
    )(amplitudes, integrals)


def solution(mesh):
    nz = mesh.shape["int"]
    nx = ny = 4
    placed = P(None, "pair", "int")
    return jax.shard_map(
        functools.partial(shards, nx=nx, ny=ny, nz=nz),
        mesh=mesh, in_specs=(placed, placed), out_specs=placed, check_vma=False,
    )
```

time: 283 us -> 77.9 us (0.28)
  waiting for transfers between devices: 243 us -> 0 us
  Pallas kernels: 0 us -> 75.1 us
  matrix products: 24.3 us -> 0 us
  between operations: 13.1 us -> 0.01 us
    reduce_scatter x2 -> x0, waiting for transfers between devices: 148 us -> none  [the longest x1 105 us: shards(): lax.psum_scatter(jnp.einsum('hak,hkb->bha', cycle_inter, row_block, preci...]
    all_gather x2 -> x0, waiting for transfers between devices: 93.4 us -> none  [the longest x1 66.6 us: shards(): lax.all_gather(amplitudes, 'pair', axis=1, tiled=True)]
    pallas_call x0 -> x1, Pallas kernels: none -> 75.1 us  [shards(): pl.pallas_call(functools.partial(kernel, nx, ny, nz), out_shape=jax.Shape...]
    dot_general x2 -> x0, matrix products: 24.3 us -> none  [the longest x1 12.8 us: shards(): jnp.einsum('hkl,hbl->hkb', lax.all_gather(amplitudes, 'pair', axis=1, til...]
  transfers between devices with their start and end apart: 4 -> 0, of which waited for: 4 -> 0; matrix products, arithmetic and copies ran while one was open for 5% -> 0% of each run, Pallas kernels for 0% -> 0%
where the time goes in v4:
time: 77.9 us; the launch traced here: 77.8 us
  Pallas kernels  75.1 us (96%)
  local copies, waits for them, and re-layouts  2.64 us (3%)
    pallas_call x1, Pallas kernels, shards(): pl.pallas_call(functools.partial(kernel, nx, ny, nz), out_shape=jax.Shape...  75.1 us
    unnamed x5, local copies, waits for them, and re-layouts  2.64 us

profile of v4, /device:TPU:1, one launch (start us, length us, event | category | flops | bytes accessed | tf_op | source)
XLA Modules:
  0.0 77.8 jit_solution(2847921748912565154)
XLA Ops:
  0.0 0.0 copy-start
  0.0 1.0 %copy-done = f32[2,96,384]{2,1,0:T(8,128)S(1)} copy-done((f32[2,96,384]{2,1,0:T(8,128)S(1)}, f32[2,96,384]{2,1,0:T(8,128)}, u32[]{:S(2)}) %copy-start) | copy-done | bytes 294936
  1.0 0.0 copy-start.1
  1.0 1.0 %copy-done.1 = f32[2,96,384]{2,1,0:T(8,128)S(1)} copy-done((f32[2,96,384]{2,1,0:T(8,128)S(1)}, f32[2,96,384]{2,1,0:T(8,128)}, u32[]{:S(2)}) %copy-start.1) | copy-done | bytes 294936
  1.9 75.1 %shard_map.28 = f32[2,96,384]{2,1,0:T(8,128)S(1)} custom-call(f32[2,96,384]{2,1,0:T(8,128)S(1)} %copy-done, f32[2,96,384]{2,1,0:T(8,128)S(1)} %copy-done.1), custom_call_target="tpu_custom_call" | custom-call | tf_op jit(solution)/shard_map/pallas_call | solution.py:203
  77.0 0.7 copy.4
Async XLA Ops:
  0.0 1.0 %copy-start = (f32[2,96,384]{2,1,0:T(8,128)S(1)}, f32[2,96,384]{2,1,0:T(8,128)}, u32[]{:S(2)}) copy-start(f32[2,96,384]{2,1,0:T(8,128)} %a_ref.1) | copy-start | bytes 884740
  1.0 1.0 %copy-start.1 = (f32[2,96,384]{2,1,0:T(8,128)S(1)}, f32[2,96,384]{2,1,0:T(8,128)}, u32[]{:S(2)}) copy-start(f32[2,96,384]{2,1,0:T(8,128)} %i_ref.1) | copy-start | bytes 884740

commit v5 on v4

--- a/solution.py
+++ b/solution.py
@@ -9,23 +9,24 @@
 
 MESH = pl.DeviceIdType.MESH
 ORDER = (
-    ("X", 1, 0), ("I", 1, 0, 0), ("X", 0, 1), ("I", 0, -1, 0), ("I", 0, 1, 0), ("X", 0, -1),
-    ("I", 0, 0, 1), ("I", 0, 0, -1), ("X", 1, 1), ("X", 1, -1), ("I", 1, 0, -1), ("I", 1, 1, 0),
-    ("I", 1, -1, 0), ("X", 0, -2), ("I", 1, 0, 1), ("I", 0, 2, 0), ("X", 0, 2), ("I", 0, -1, 1),
-    ("I", 0, -1, -1), ("I", 0, 1, -1), ("I", 0, 1, 1), ("I", 0, 0, 2), ("X", 1, 2), ("X", 1, -2),
-    ("I", 1, 1, 1), ("I", 1, -1, 1), ("X", 0, -3), ("X", 0, 3), ("I", 1, 1, -1), ("I", 1, 0, 2),
-    ("I", 1, 2, 0), ("I", 1, -1, -1), ("I", 1, 1, 2), ("X", 1, 3), ("I", 0, 2, 1), ("X", 1, -3),
-    ("I", 1, -1, 2), ("I", 0, 2, -1), ("X", 0, 4), ("I", 1, 2, -1), ("I", 1, 2, 1), ("I", 0, -1, 2),
-    ("own",), ("X", 1, 4), ("I", 0, 1, 2), ("I", 1, 2, 2), ("I", 0, 2, 2), ("comp", 1),
-    ("A", 0, -1, 0), ("A", 0, 1, 0), ("A", 0, 0, 1), ("A", 0, 0, -1), ("A", 1, 0, 0), ("comp", 0),
-    ("T", 1, 1), ("T", 1, -1), ("A", 1, 0, 1), ("A", 1, 1, 0), ("A", 1, -1, 0), ("A", 1, 0, -1),
-    ("A", 0, 2, 0), ("T", 0, -1), ("T", 0, 1), ("A", 0, -1, 1), ("A", 0, -1, -1), ("A", 0, 1, -1),
-    ("A", 0, 1, 1), ("A", 1, 0, 2), ("T", 1, -2), ("T", 1, 2), ("A", 0, 0, 2), ("A", 1, 1, -1),
-    ("T", 0, -2), ("T", 0, 2), ("A", 1, 1, 1), ("A", 1, 2, 0), ("A", 1, -1, 1), ("A", 1, -1, -1),
-    ("T", 1, 3), ("T", 1, -3), ("A", 0, 2, 1), ("A", 0, 2, -1), ("A", 1, 1, 2), ("A", 0, -1, 2),
-    ("A", 1, 2, 1), ("T", 0, -3), ("T", 0, 3), ("A", 1, 2, -1), ("A", 1, -1, 2), ("A", 0, 1, 2),
-    ("A", 1, 2, 2), ("T", 1, 4), ("A", 0, 2, 2), ("R", 1), ("R", -3), ("R", 2), ("R", -2), ("R", 0),
-    ("R", -1), ("R", 3), ("T", 0, 4), ("R", 4),
+    ("own", "I", 1), ("own", "X"), ("own", "I", 2), ("I", 0, 1, 0), ("I", 1, 1, 0), ("I", 0, -1, 0),
+    ("X", 1, -1), ("X", 1, 1), ("X", 0, -1), ("X", 0, 1), ("I", 1, -1, 0), ("I", 0, 0, -1),
+    ("I", 0, 2, 0), ("I", 1, 0, -1), ("X", 1, -2), ("I", 0, 1, -1), ("I", 0, 1, 1), ("I", 1, 2, 0),
+    ("X", 1, 2), ("I", 1, 1, 1), ("I", 0, -1, 1), ("X", 0, 2), ("I", 1, -1, 1), ("X", 0, -2),
+    ("I", 0, -1, -1), ("I", 0, 0, 1), ("I", 1, 0, 1), ("I", 0, 2, 1), ("X", 1, -3), ("X", 1, 3),
+    ("I", 1, 2, 1), ("X", 1, 0), ("X", 0, 3), ("I", 1, 1, -1), ("own", "A", 1), ("I", 0, 1, 2),
+    ("I", 1, 0, 0), ("I", 0, 2, -1), ("I", 1, 2, -1), ("I", 1, 1, 2), ("own", "A", 2),
+    ("I", 1, -1, 2), ("X", 0, -3), ("I", 0, -1, 2), ("X", 1, 4), ("I", 1, -1, -1), ("I", 1, 0, 2),
+    ("I", 0, 0, 2), ("X", 0, 4), ("I", 1, 2, 2), ("I", 0, 2, 2), ("comp", 1), ("A", 0, 1, 0),
+    ("comp", 0), ("A", 1, 1, 0), ("A", 0, -1, 0), ("T", 1, 1), ("T", 0, 1), ("A", 0, 2, 0),
+    ("T", 0, -1), ("A", 1, -1, 0), ("A", 1, 2, 0), ("A", 1, 1, 1), ("A", 0, 0, -1), ("T", 1, -1),
+    ("A", 1, 0, 1), ("A", 0, -1, 1), ("A", 0, 1, -1), ("T", 1, 2), ("T", 0, 2), ("A", 0, 1, 1),
+    ("A", 0, -1, -1), ("T", 0, -2), ("A", 1, -1, 1), ("A", 1, 2, 1), ("T", 1, -2), ("A", 0, 0, 1),
+    ("A", 1, 0, -1), ("A", 1, -1, -1), ("A", 0, 2, -1), ("A", 1, 1, -1), ("A", 0, 2, 1),
+    ("A", 0, -1, 2), ("A", 1, 2, -1), ("A", 1, 0, 0), ("T", 1, 3), ("A", 1, 0, 2), ("T", 0, 3),
+    ("T", 0, -3), ("A", 1, 1, 2), ("A", 0, 1, 2), ("A", 1, -1, 2), ("A", 0, 0, 2), ("T", 1, -3),
+    ("A", 1, 2, 2), ("A", 0, 2, 2), ("R", -1), ("R", 3), ("R", 2), ("R", 0), ("R", -3), ("R", 1),
+    ("T", 1, 4), ("R", -2), ("T", 0, 4), ("R", 4),
 )
 
 
@@ -115,20 +116,15 @@
     def turn(part, first, second):
         return first * (1 - part) + second * part, first * part + second * (1 - part)
 
-    def xy_own(ref, buf, sems, high, low):
+    def xy_own(ref, buf, sems, high, low, leg):
         slot, sem = buf.at[here, c], sems.at[c, here]
-
-        def out(first, second):
-            dx, dy = turn(c, first, second)
+        for d in (s, -s):
+            dx, dy = turn(c, d, 0) if leg == 1 else turn(c, 0, d)
             for h in (c, 1 - c):
                 send(ref.at[h], slot, sem, device(dx, dy, 0, h))
-
-        out(s, 0)
-        out(-s, 0)
-        send(ref.at[1 - c], slot, sem, sibling)
-        out(0, s)
-        out(0, -s)
-        keep(ref[c], high, low, here, c)
+        if leg == 1:
+            send(ref.at[1 - c], slot, sem, sibling)
+            keep(ref[c], high, low, here, c)
 
     def xy_event(buf, sems, high, low, own, first, second):
         part = parts[own]
@@ -170,19 +166,23 @@
         t = [v[at].reshape(2 * rows, width) for v in (t_high, t_low)]
         total[...] += product(t, (block(a_high, at), block(a_low, at)))
 
-    z_first()
-    xy_own(i_ref, i_cols, i_sem, i_high, i_low)
+    i_all = (i_cols, i_sem, i_high, i_low)
+    a_all = (a_cols, a_sem, a_high, a_low)
     for name, *what in ORDER:
         if name == "X":
             z_event(x_rows, x_sem, x_high, x_low, *what)
         elif name == "T":
             z_event(t_rows, t_sem, t_high, t_low, *what)
         elif name == "I":
-            xy_event(i_cols, i_sem, i_high, i_low, *what)
+            xy_event(*i_all, *what)
         elif name == "A":
-            xy_event(a_cols, a_sem, a_high, a_low, *what)
+            xy_event(*a_all, *what)
+        elif name == "own" and what[0] == "X":
+            z_first()
+        elif name == "own" and what[0] == "I":
+            xy_own(i_ref, *i_all, what[1])
         elif name == "own":
-            xy_own(a_ref, a_cols, a_sem, a_high, a_low)
+            xy_own(a_ref, *a_all, what[1])
         elif name == "comp":
             t_event(*what)
         else:

time: 77.9 us -> 72 us (0.924)
  Pallas kernels: 75.1 us -> 69.2 us
    pallas_call x1, Pallas kernels: 75.1 us -> 69.2 us  [shards(): pl.pallas_call(functools.partial(kernel, nx, ny, nz), out_shape=jax.Shape...]
where the time goes in v5:
time: 72 us; the launch traced here: 71.8 us
  Pallas kernels  69.2 us (96%)
  local copies, waits for them, and re-layouts  2.64 us (4%)
    pallas_call x1, Pallas kernels, shards(): pl.pallas_call(functools.partial(kernel, nx, ny, nz), out_shape=jax.Shape...  69.2 us
    unnamed x5, local copies, waits for them, and re-layouts  2.64 us

profile of v5, /device:TPU:1, one launch (start us, length us, event | category | flops | bytes accessed | tf_op | source)
XLA Modules:
  0.0 71.8 jit_solution(1714608693643364267)
XLA Ops:
  0.0 0.0 copy-start
  0.0 1.0 %copy-done = f32[2,96,384]{2,1,0:T(8,128)S(1)} copy-done((f32[2,96,384]{2,1,0:T(8,128)S(1)}, f32[2,96,384]{2,1,0:T(8,128)}, u32[]{:S(2)}) %copy-start) | copy-done | bytes 294936
  1.0 0.0 copy-start.1
  1.0 1.0 %copy-done.1 = f32[2,96,384]{2,1,0:T(8,128)S(1)} copy-done((f32[2,96,384]{2,1,0:T(8,128)S(1)}, f32[2,96,384]{2,1,0:T(8,128)}, u32[]{:S(2)}) %copy-start.1) | copy-done | bytes 294936
  1.9 69.2 %shard_map.28 = f32[2,96,384]{2,1,0:T(8,128)S(1)} custom-call(f32[2,96,384]{2,1,0:T(8,128)S(1)} %copy-done, f32[2,96,384]{2,1,0:T(8,128)S(1)} %copy-done.1), custom_call_target="tpu_custom_call" | custom-call | tf_op jit(solution)/shard_map/pallas_call | solution.py:203
  71.1 0.7 copy.4
Async XLA Ops:
  0.0 1.0 %copy-start = (f32[2,96,384]{2,1,0:T(8,128)S(1)}, f32[2,96,384]{2,1,0:T(8,128)}, u32[]{:S(2)}) copy-start(f32[2,96,384]{2,1,0:T(8,128)} %a_ref.1) | copy-start | bytes 884740
  1.0 1.0 %copy-start.1 = (f32[2,96,384]{2,1,0:T(8,128)S(1)}, f32[2,96,384]{2,1,0:T(8,128)}, u32[]{:S(2)}) copy-start(f32[2,96,384]{2,1,0:T(8,128)} %i_ref.1) | copy-start | bytes 884740

commit v6 on v5

--- a/solution.py
+++ b/solution.py
@@ -9,24 +9,24 @@
 
 MESH = pl.DeviceIdType.MESH
 ORDER = (
-    ("own", "I", 1), ("own", "X"), ("own", "I", 2), ("I", 0, 1, 0), ("I", 1, 1, 0), ("I", 0, -1, 0),
-    ("X", 1, -1), ("X", 1, 1), ("X", 0, -1), ("X", 0, 1), ("I", 1, -1, 0), ("I", 0, 0, -1),
-    ("I", 0, 2, 0), ("I", 1, 0, -1), ("X", 1, -2), ("I", 0, 1, -1), ("I", 0, 1, 1), ("I", 1, 2, 0),
-    ("X", 1, 2), ("I", 1, 1, 1), ("I", 0, -1, 1), ("X", 0, 2), ("I", 1, -1, 1), ("X", 0, -2),
-    ("I", 0, -1, -1), ("I", 0, 0, 1), ("I", 1, 0, 1), ("I", 0, 2, 1), ("X", 1, -3), ("X", 1, 3),
-    ("I", 1, 2, 1), ("X", 1, 0), ("X", 0, 3), ("I", 1, 1, -1), ("own", "A", 1), ("I", 0, 1, 2),
-    ("I", 1, 0, 0), ("I", 0, 2, -1), ("I", 1, 2, -1), ("I", 1, 1, 2), ("own", "A", 2),
-    ("I", 1, -1, 2), ("X", 0, -3), ("I", 0, -1, 2), ("X", 1, 4), ("I", 1, -1, -1), ("I", 1, 0, 2),
-    ("I", 0, 0, 2), ("X", 0, 4), ("I", 1, 2, 2), ("I", 0, 2, 2), ("comp", 1), ("A", 0, 1, 0),
-    ("comp", 0), ("A", 1, 1, 0), ("A", 0, -1, 0), ("T", 1, 1), ("T", 0, 1), ("A", 0, 2, 0),
-    ("T", 0, -1), ("A", 1, -1, 0), ("A", 1, 2, 0), ("A", 1, 1, 1), ("A", 0, 0, -1), ("T", 1, -1),
-    ("A", 1, 0, 1), ("A", 0, -1, 1), ("A", 0, 1, -1), ("T", 1, 2), ("T", 0, 2), ("A", 0, 1, 1),
-    ("A", 0, -1, -1), ("T", 0, -2), ("A", 1, -1, 1), ("A", 1, 2, 1), ("T", 1, -2), ("A", 0, 0, 1),
-    ("A", 1, 0, -1), ("A", 1, -1, -1), ("A", 0, 2, -1), ("A", 1, 1, -1), ("A", 0, 2, 1),
-    ("A", 0, -1, 2), ("A", 1, 2, -1), ("A", 1, 0, 0), ("T", 1, 3), ("A", 1, 0, 2), ("T", 0, 3),
-    ("T", 0, -3), ("A", 1, 1, 2), ("A", 0, 1, 2), ("A", 1, -1, 2), ("A", 0, 0, 2), ("T", 1, -3),
-    ("A", 1, 2, 2), ("A", 0, 2, 2), ("R", -1), ("R", 3), ("R", 2), ("R", 0), ("R", -3), ("R", 1),
-    ("T", 1, 4), ("R", -2), ("T", 0, 4), ("R", 4),
+    ("own", "I", 2), ("own", "I", 1), ("own", "X"), ("I", 0, 1, 0), ("X", 0, -1), ("X", 0, 1),
+    ("I", 1, 1, 0), ("I", 1, -1, 0), ("X", 1, -1), ("I", 0, -1, 0), ("X", 1, 1), ("X", 0, -2),
+    ("I", 0, 2, 0), ("X", 0, 2), ("I", 1, 2, 0), ("X", 1, 2), ("I", 1, 0, 0), ("X", 1, 0),
+    ("I", 0, -1, -1), ("X", 1, -2), ("I", 0, 0, 1), ("I", 1, 1, 1), ("I", 0, 0, -1),
+    ("I", 1, -1, -1), ("I", 1, 0, 1), ("I", 0, 1, 1), ("I", 1, 1, -1), ("X", 0, 3), ("I", 0, 2, 1),
+    ("I", 0, 1, -1), ("I", 1, 2, 1), ("I", 0, 2, -1), ("X", 1, 3), ("I", 0, -1, 1), ("I", 1, 0, -1),
+    ("own", "A", 2), ("I", 1, -1, 1), ("own", "A", 1), ("X", 0, -3), ("I", 1, -1, 2),
+    ("I", 0, -1, 2), ("I", 1, 2, -1), ("I", 0, 0, 2), ("A", 1, 0, 0), ("I", 1, 0, 2), ("X", 1, -3),
+    ("X", 0, 4), ("I", 0, 1, 2), ("X", 1, 4), ("I", 1, 1, 2), ("I", 0, 2, 2), ("I", 1, 2, 2),
+    ("comp", 1), ("A", 0, 1, 0), ("comp", 0), ("A", 1, 1, 0), ("A", 0, -1, 0), ("A", 1, -1, 0),
+    ("T", 1, 1), ("T", 1, -1), ("T", 0, 1), ("A", 0, 1, 1), ("A", 0, 0, -1), ("A", 0, 2, 0),
+    ("A", 1, 1, 1), ("A", 1, 2, 0), ("T", 0, -1), ("A", 1, 1, -1), ("A", 1, 0, 1), ("T", 1, 2),
+    ("A", 0, 0, 1), ("A", 0, 1, -1), ("A", 0, -1, -1), ("T", 0, 2), ("A", 1, -1, -1), ("T", 1, -2),
+    ("A", 0, 2, 1), ("A", 1, 2, 1), ("A", 0, -1, 1), ("T", 0, -2), ("T", 1, 3), ("A", 1, 0, -1),
+    ("A", 1, 1, 2), ("A", 0, 2, -1), ("T", 0, 3), ("A", 0, 1, 2), ("A", 0, -1, 2), ("A", 1, 2, -1),
+    ("A", 1, -1, 1), ("A", 0, 0, 2), ("A", 1, 2, 2), ("A", 0, 2, 2), ("A", 1, -1, 2), ("T", 1, -3),
+    ("A", 1, 0, 2), ("T", 0, -3), ("R", 2), ("R", -2), ("R", 0), ("R", -1), ("R", 1), ("R", 3),
+    ("R", -3), ("T", 1, 4), ("T", 0, 4), ("R", 4),
 )
 
 
@@ -104,13 +104,15 @@
         keep(a_ref[c], x_high, x_low, z, c)
 
     def z_event(buf, sems, high, low, own, k):
-        at, part = zs(-s * k), parts[own]
+        part = parts[own]
+        way = 1 - 2 * part
+        at = zs(-way * k)
         slot, sem = buf.at[at, part], sems.at[part, at]
         arrived(slot, sem)
         if 0 < k < far:
-            send(slot, slot, sem, device(0, 0, s, c))
+            send(slot, slot, sem, device(0, 0, way, c))
         elif 1 - far < k < 0:
-            send(slot, slot, sem, device(0, 0, -s, c))
+            send(slot, slot, sem, device(0, 0, -way, c))
         keep(buf[at, part], high, low, at, part)
 
     def turn(part, first, second):
@@ -136,8 +138,8 @@
         if second == 0 and first != 0:
             along = [(s, 0)] if first == 1 else []
             along += [(0, s), (0, -s)]
-        elif second == 1:
-            along = [(0, s)]
+        elif second == (1 if first in (0, 2) else -1):
+            along = [(0, second * s)]
         for f, g in along:
             dx, dy = turn(part, f, g)
             send(slot, slot, sem, device(dx, dy, 0, c))
@@ -157,14 +159,17 @@
         total[at, :] = value
         t_rows[z, part] = value
         slot, sem = t_rows.at[z, part], t_sem.at[part, z]
-        send(slot, slot, sem, device(0, 0, s, c))
-        send(slot, slot, sem, device(0, 0, -s, c))
+        way = 1 - 2 * part
+        send(slot, slot, sem, device(0, 0, way, c))
+        send(slot, slot, sem, device(0, 0, -way, c))
         keep(value, t_high, t_low, z, part)
 
-    def r_event(k):
-        at = zs(-s * k)
-        t = [v[at].reshape(2 * rows, width) for v in (t_high, t_low)]
-        total[...] += product(t, (block(a_high, at), block(a_low, at)))
+    def r_event(k, own=1):
+        at, part = zs(-s * k), parts[own]
+        here_rows = pl.ds(pl.multiple_of(part * rows, rows), rows)
+        total[here_rows, :] += product(
+            (t_high[at, part], t_low[at, part]), (block(a_high, at), block(a_low, at))
+        )
 
     i_all = (i_cols, i_sem, i_high, i_low)
     a_all = (a_cols, a_sem, a_high, a_low)
@@ -189,6 +194,9 @@
             r_event(*what)
     part = pl.ds(pl.multiple_of((1 - c) * rows, rows), rows)
     send(total.at[part], theirs, r_sem, sibling)
+    for name, *what in ORDER:
+        if name == "R":
+            r_event(*what, own=0)
     o_ref[c] = total[pl.ds(pl.multiple_of(c * rows, rows), rows), :]
     arrived(theirs, r_sem)
     o_ref[1 - c] = theirs[...]

time: 72 us -> 70.4 us (0.978)
  Pallas kernels: 69.2 us -> 67.4 us
    pallas_call x1, Pallas kernels: 69.2 us -> 67.4 us  [shards(): pl.pallas_call(functools.partial(kernel, nx, ny, nz), out_shape=jax.Shape...]
where the time goes in v6:
time: 70.4 us; the launch traced here: 70 us
  Pallas kernels  67.4 us (96%)
  local copies, waits for them, and re-layouts  2.64 us (4%)
    pallas_call x1, Pallas kernels, shards(): pl.pallas_call(functools.partial(kernel, nx, ny, nz), out_shape=jax.Shape...  67.4 us
    unnamed x5, local copies, waits for them, and re-layouts  2.64 us

profile of v6, /device:TPU:1, one launch (start us, length us, event | category | flops | bytes accessed | tf_op | source)
XLA Modules:
  0.0 70.0 jit_solution(302552084788459191)
XLA Ops:
  0.0 0.0 copy-start
  0.0 1.0 %copy-done = f32[2,96,384]{2,1,0:T(8,128)S(1)} copy-done((f32[2,96,384]{2,1,0:T(8,128)S(1)}, f32[2,96,384]{2,1,0:T(8,128)}, u32[]{:S(2)}) %copy-start) | copy-done | bytes 294936
  1.0 0.0 copy-start.1
  1.0 1.0 %copy-done.1 = f32[2,96,384]{2,1,0:T(8,128)S(1)} copy-done((f32[2,96,384]{2,1,0:T(8,128)S(1)}, f32[2,96,384]{2,1,0:T(8,128)}, u32[]{:S(2)}) %copy-start.1) | copy-done | bytes 294936
  1.9 67.4 %shard_map.28 = f32[2,96,384]{2,1,0:T(8,128)S(1)} custom-call(f32[2,96,384]{2,1,0:T(8,128)S(1)} %copy-done, f32[2,96,384]{2,1,0:T(8,128)S(1)} %copy-done.1), custom_call_target="tpu_custom_call" | custom-call | tf_op jit(solution)/shard_map/pallas_call | solution.py:211
  69.3 0.7 %copy.4 = f32[2,96,384]{2,1,0:T(8,128)} copy(f32[2,96,384]{2,1,0:T(8,128)S(1)} %shard_map.28) | data formatting | bytes 589824
Async XLA Ops:
  0.0 1.0 %copy-start = (f32[2,96,384]{2,1,0:T(8,128)S(1)}, f32[2,96,384]{2,1,0:T(8,128)}, u32[]{:S(2)}) copy-start(f32[2,96,384]{2,1,0:T(8,128)} %a_ref.1) | copy-start | bytes 884740
  1.0 1.0 %copy-start.1 = (f32[2,96,384]{2,1,0:T(8,128)S(1)}, f32[2,96,384]{2,1,0:T(8,128)}, u32[]{:S(2)}) copy-start(f32[2,96,384]{2,1,0:T(8,128)} %i_ref.1) | copy-start | bytes 884740

commit v7 on v6

--- a/solution.py
+++ b/solution.py
@@ -37,7 +37,9 @@
 
 def product(a, b):
     dot = functools.partial(jnp.dot, preferred_element_type=jnp.float32)
-    return dot(a[0], b[0]) + (dot(a[0], b[1]) + dot(a[1], b[0]))
+    n = a[0].shape[0]
+    both = dot(jnp.concatenate(a, axis=0), b[0])
+    return both[:n] + (dot(a[0], b[1]) + both[n:])
 
 
 def kernel(
@@ -94,9 +96,10 @@
         return lax.rem(z + d + nz, nz)
 
     far = nz // 2
+    pieces = ((slice(0, rows // 2), 0), (slice(rows // 2, rows), 1))
 
     def z_first():
-        slot, sem = x_rows.at[z, c], x_sem.at[c, z]
+        slot, sem = x_rows.at[z, c], x_sem.at[c, z, 0]
         for d in (s, -s):
             for h in (c, 1 - c):
                 send(a_ref.at[h], slot, sem, device(0, 0, d, h))
@@ -107,12 +110,13 @@
         part = parts[own]
         way = 1 - 2 * part
         at = zs(-way * k)
-        slot, sem = buf.at[at, part], sems.at[part, at]
-        arrived(slot, sem)
-        if 0 < k < far:
-            send(slot, slot, sem, device(0, 0, way, c))
-        elif 1 - far < k < 0:
-            send(slot, slot, sem, device(0, 0, -way, c))
+        for rows_at, half in pieces if buf is t_rows else ((slice(None), 0),):
+            slot, sem = buf.at[at, part, rows_at], sems.at[part, at, half]
+            arrived(slot, sem)
+            if 0 < k < far:
+                send(slot, slot, sem, device(0, 0, way, c))
+            elif 1 - far < k < 0:
+                send(slot, slot, sem, device(0, 0, -way, c))
         keep(buf[at, part], high, low, at, part)
 
     def turn(part, first, second):
@@ -158,10 +162,11 @@
             )
         total[at, :] = value
         t_rows[z, part] = value
-        slot, sem = t_rows.at[z, part], t_sem.at[part, z]
         way = 1 - 2 * part
-        send(slot, slot, sem, device(0, 0, way, c))
-        send(slot, slot, sem, device(0, 0, -way, c))
+        for rows_at, half in pieces:
+            slot, sem = t_rows.at[z, part, rows_at], t_sem.at[part, z, half]
+            send(slot, slot, sem, device(0, 0, way, c))
+            send(slot, slot, sem, device(0, 0, -way, c))
         keep(value, t_high, t_low, z, part)
 
     def r_event(k, own=1):
@@ -228,11 +233,11 @@
             pltpu.VMEM((nx * ny, 2, rows, width), b16),
             pltpu.VMEM((nz, 2, rows, width), b16),
             pltpu.VMEM((nz, 2, rows, width), b16),
-            dma((128,)),
-            dma((2, nz)),
+            dma((160,)),
+            dma((2, nz, 2)),
             dma((2, nx * ny)),
             dma((2, nx * ny)),
-            dma((2, nz)),
+            dma((2, nz, 2)),
             dma,
         ],
         compiler_params=pltpu.CompilerParams(

time: 70.4 us -> 69.7 us (0.990)
  no operation moved by 1% of the time
where the time goes in v7:
time: 69.7 us; the launch traced here: 69.4 us
  Pallas kernels  66.8 us (96%)
  local copies, waits for them, and re-layouts  2.64 us (4%)
    pallas_call x1, Pallas kernels, shards(): pl.pallas_call(functools.partial(kernel, nx, ny, nz), out_shape=jax.Shape...  66.8 us
    unnamed x5, local copies, waits for them, and re-layouts  2.64 us

profile of v7, /device:TPU:1, one launch (start us, length us, event | category | flops | bytes accessed | tf_op | source)
XLA Modules:
  0.0 69.4 jit_solution(10376945761680893745)
XLA Ops:
  0.0 0.0 copy-start
  0.0 1.0 %copy-done = f32[2,96,384]{2,1,0:T(8,128)S(1)} copy-done((f32[2,96,384]{2,1,0:T(8,128)S(1)}, f32[2,96,384]{2,1,0:T(8,128)}, u32[]{:S(2)}) %copy-start) | copy-done | bytes 294936
  1.0 0.0 copy-start.1
  1.0 1.0 %copy-done.1 = f32[2,96,384]{2,1,0:T(8,128)S(1)} copy-done((f32[2,96,384]{2,1,0:T(8,128)S(1)}, f32[2,96,384]{2,1,0:T(8,128)}, u32[]{:S(2)}) %copy-start.1) | copy-done | bytes 294936
  1.9 66.8 %shard_map.28 = f32[2,96,384]{2,1,0:T(8,128)S(1)} custom-call(f32[2,96,384]{2,1,0:T(8,128)S(1)} %copy-done, f32[2,96,384]{2,1,0:T(8,128)S(1)} %copy-done.1), custom_call_target="tpu_custom_call" | custom-call | tf_op jit(solution)/shard_map/pallas_call | solution.py:216
  68.7 0.7 %copy.4 = f32[2,96,384]{2,1,0:T(8,128)} copy(f32[2,96,384]{2,1,0:T(8,128)S(1)} %shard_map.28) | data formatting | bytes 589824
Async XLA Ops:
  0.0 1.0 %copy-start = (f32[2,96,384]{2,1,0:T(8,128)S(1)}, f32[2,96,384]{2,1,0:T(8,128)}, u32[]{:S(2)}) copy-start(f32[2,96,384]{2,1,0:T(8,128)} %a_ref.1) | copy-start | bytes 884740
  1.0 1.0 %copy-start.1 = (f32[2,96,384]{2,1,0:T(8,128)S(1)}, f32[2,96,384]{2,1,0:T(8,128)}, u32[]{:S(2)}) copy-start(f32[2,96,384]{2,1,0:T(8,128)} %i_ref.1) | copy-start | bytes 884740

commit v8 on v7

--- a/solution.py
+++ b/solution.py
@@ -44,7 +44,7 @@
 
 def kernel(
     nx, ny, nz, a_ref, i_ref, o_ref,
-    x_rows, i_cols, a_cols, t_rows, total, theirs,
+    x_rows, i_cols, a_cols, t_rows, total,
     x_high, x_low, i_high, i_low, a_high, a_low, t_high, t_low,
     send_sem, x_sem, i_sem, a_sem, t_sem, r_sem,
 ):
@@ -198,13 +198,12 @@
         else:
             r_event(*what)
     part = pl.ds(pl.multiple_of((1 - c) * rows, rows), rows)
-    send(total.at[part], theirs, r_sem, sibling)
+    send(total.at[part], o_ref.at[c], r_sem, sibling)
     for name, *what in ORDER:
         if name == "R":
             r_event(*what, own=0)
     o_ref[c] = total[pl.ds(pl.multiple_of(c * rows, rows), rows), :]
-    arrived(theirs, r_sem)
-    o_ref[1 - c] = theirs[...]
+    arrived(o_ref.at[1 - c], r_sem)
     for copy in started:
         copy.wait_send()
 
@@ -224,7 +223,6 @@
             pltpu.VMEM((nx * ny, 2, rows, width), f32),
             pltpu.VMEM((nz, 2, rows, width), f32),
             pltpu.VMEM((2 * rows, width), f32),
-            pltpu.VMEM((rows, width), f32),
             pltpu.VMEM((nz, 2, rows, width), b16),
             pltpu.VMEM((nz, 2, rows, width), b16),
             pltpu.VMEM((nx * ny, 2, rows, width), b16),

time: 69.7 us -> 69.7 us (level)
  no operation moved by 1% of the time
where the time goes in v8:
time: 69.7 us; the launch traced here: 69.4 us
  Pallas kernels  66.7 us (96%)
  local copies, waits for them, and re-layouts  2.64 us (4%)
    pallas_call x1, Pallas kernels, shards(): pl.pallas_call(functools.partial(kernel, nx, ny, nz), out_shape=jax.Shape...  66.7 us
    unnamed x5, local copies, waits for them, and re-layouts  2.64 us

profile of v8, /device:TPU:1, one launch (start us, length us, event | category | flops | bytes accessed | tf_op | source)
XLA Modules:
  0.0 69.4 jit_solution(9189489709465615150)
XLA Ops:
  0.0 0.0 copy-start
  0.0 1.0 %copy-done = f32[2,96,384]{2,1,0:T(8,128)S(1)} copy-done((f32[2,96,384]{2,1,0:T(8,128)S(1)}, f32[2,96,384]{2,1,0:T(8,128)}, u32[]{:S(2)}) %copy-start) | copy-done | bytes 294936
  1.0 0.0 copy-start.1
  1.0 1.0 %copy-done.1 = f32[2,96,384]{2,1,0:T(8,128)S(1)} copy-done((f32[2,96,384]{2,1,0:T(8,128)S(1)}, f32[2,96,384]{2,1,0:T(8,128)}, u32[]{:S(2)}) %copy-start.1) | copy-done | bytes 294936
  1.9 66.7 %shard_map.28 = f32[2,96,384]{2,1,0:T(8,128)S(1)} custom-call(f32[2,96,384]{2,1,0:T(8,128)S(1)} %copy-done, f32[2,96,384]{2,1,0:T(8,128)S(1)} %copy-done.1), custom_call_target="tpu_custom_call" | custom-call | tf_op jit(solution)/shard_map/pallas_call | solution.py:215
  68.7 0.7 %copy.4 = f32[2,96,384]{2,1,0:T(8,128)} copy(f32[2,96,384]{2,1,0:T(8,128)S(1)} %shard_map.28) | data formatting | bytes 589824
Async XLA Ops:
  0.0 1.0 %copy-start = (f32[2,96,384]{2,1,0:T(8,128)S(1)}, f32[2,96,384]{2,1,0:T(8,128)}, u32[]{:S(2)}) copy-start(f32[2,96,384]{2,1,0:T(8,128)} %a_ref.1) | copy-start | bytes 884740
  1.0 1.0 %copy-start.1 = (f32[2,96,384]{2,1,0:T(8,128)S(1)}, f32[2,96,384]{2,1,0:T(8,128)}, u32[]{:S(2)}) copy-start(f32[2,96,384]{2,1,0:T(8,128)} %i_ref.1) | copy-start | bytes 884740
